TPU v7x, 32 devices: a whole 2x2x4 slice. The times are simulated.
32 devices in a mesh: wall: 8 (over z, x), stream: 4 (over y, core).
Axes of the slice: x: 2, y: 2, z: 4, core: 2. Of those that a mesh axis runs over, the one named last changes fastest.
Arguments:
- dist: float32 [8, 64, 32, 1024], P(None, None, 'stream', 'wall'), may hold values from 0.25 to 4
- quad_weight: float32 [8, 64], replicated, may hold values from 0.0009765625 to 0.00390625
- vel_x: float32 [64], replicated, may hold values from -3 to 3
- vel_y: float32 [8], replicated, may hold values from -3 to 3, as said below
- flags: int32 [32, 1024], P('stream', 'wall'), may hold values from 0 to 2
- block_inverse: float32 [8, 128, 128], replicated, as said below
- line_coupling: float32 [8], replicated, as said below
Outputs:
- advanced: float32 [8, 64, 32, 1024], P(None, None, 'stream', 'wall')
Inputs may be any that keep to these rules, and one draw needn't show every extreme that they name: vel_y[g] is positive for g < 4 and negative otherwise. block_inverse[g] is zero above the diagonal for g < 4 and zero below it otherwise; no entry is negative. line_coupling[g] times the entry of block_inverse[g] that links the last node of a block to the first node of the next (row 127, column 0 for g < 4; row 0, column 127 otherwise) is positive and below 1.
All inputs are finite; a program needn't handle non-finite values.
Results may differ from a plain program's by a relative error of at most 0.00023.
Values sent between devices are 32-bit elements; how exact they have to be, the bound alone decides.
A program may use at most 64 MiB of HBM per device.

v0:
```python
import jax
import jax.numpy as jnp
from jax import lax
from jax.sharding import PartitionSpec as P

ITERS = 2


CFL_STREAM = 0.12
RELAX = 0.3
PENALTY = 0.5
INLET_SPEED = 0.5


def with_halo(block, sides, width):
    for axis, dim in sides:
        count = lax.axis_size(axis)
        forward = [(i, i + 1) for i in range(count - 1)]
        forward.append((count - 1, 0))
        backward = [(target, source) for source, target in forward]
        low = lax.ppermute(
            lax.slice_in_dim(block, block.shape[dim] - width, None, axis=dim), axis, forward
        )
        high = lax.ppermute(lax.slice_in_dim(block, 0, width, axis=dim), axis, backward)
        block = jnp.concatenate([low, block, high], axis=dim)
    return block


def on_device(dist, quad_weight, vel_x, vel_y, flags, block_inverse, line_coupling):
    highest = lax.Precision.HIGHEST
    half_groups = dist.shape[0] // 2
    block_len = dist.shape[3]
    square_y = vel_y[:, None] * vel_y[:, None]
    rest_table = jnp.exp(-(vel_x[None, :] * vel_x[None, :] + square_y) / 2.0)
    shifted = vel_x[None, :] - INLET_SPEED
    inlet_table = jnp.exp(-(shifted * shifted + square_y) / 2.0)
    rest_table = rest_table / jnp.sum(quad_weight * rest_table)
    inlet_table = inlet_table / jnp.sum(quad_weight * inlet_table)
    solid = (flags == 1).astype(jnp.float32)
    inflow = (flags == 2).astype(jnp.float32)
    moment_table = jnp.stack(
        [quad_weight, quad_weight * vel_x[None, :], quad_weight * vel_y[:, None]]
    )
    speed_column = vel_x[None, :, None, None]
    vertical_column = vel_y[:, None, None, None]
    factor_down = (line_coupling[:half_groups] * block_inverse[:half_groups, block_len - 1, 0])[
        :, None
    ]
    factor_up = (line_coupling[half_groups:] * block_inverse[half_groups:, 0, block_len - 1])[
        :, None
    ]
    spike_down = line_coupling[:half_groups, None] * block_inverse[:half_groups, :, 0]
    spike_up = line_coupling[half_groups:, None] * block_inverse[half_groups:, :, block_len - 1]
    current = dist
    for sweep in range(ITERS):
        moments = jnp.einsum("mgx,gxsw->msw", moment_table, current, precision=highest)
        density = moments[0]
        speed_x = moments[1] / density
        speed_y = moments[2] / density
        diff_x = speed_column - speed_x[None, None]
        diff_y = vertical_column - speed_y[None, None]
        exponent = jnp.exp(-(diff_x * diff_x + diff_y * diff_y) / 2.0)
        zsum = jnp.einsum("gx,gxsw->sw", quad_weight, exponent, precision=highest)
        equil = density[None, None] * exponent / zsum[None, None]
        edges = with_halo(current, (("stream", 2),), 1)
        left_side = edges[:, :, :-2]
        right_side = edges[:, :, 2:]
        upwind = jnp.maximum(speed_column, 0.0) * (current - left_side) + jnp.minimum(
            speed_column, 0.0
        ) * (right_side - current)
        boundary = solid[None, None] * (
            density[None, None] * rest_table[:, :, None, None] - current
        ) + inflow[None, None] * (inlet_table[:, :, None, None] - current)
        rhs = current - CFL_STREAM * upwind + RELAX * equil + PENALTY * boundary
        solved = jnp.einsum("gxsj,gij->gxsi", rhs, block_inverse, precision=highest)
        ends_down = solved[:half_groups, :, :, block_len - 1].reshape(half_groups, -1)
        ends_up = solved[half_groups:, :, :, 0].reshape(rhs.shape[0] - half_groups, -1)
        stacked = jnp.stack([ends_down, ends_up])[None]
        collected = lax.all_gather(stacked, "wall", axis=0, tiled=True)
        position = lax.axis_index("wall").astype(jnp.float32)
        order = jnp.arange(lax.axis_size("wall")).astype(jnp.float32)
        gap_down = position - 1.0 - order
        gap_up = order - position - 1.0
        weight_down = jnp.where(
            gap_down[None] >= 0.0,
            jnp.exp(jnp.maximum(gap_down, 0.0)[None] * jnp.log(factor_down)),
            0.0,
        )
        weight_up = jnp.where(
            gap_up[None] >= 0.0, jnp.exp(jnp.maximum(gap_up, 0.0)[None] * jnp.log(factor_up)), 0.0
        )
        before_down = jnp.einsum("gq,qgm->gm", weight_down, collected[:, 0], precision=highest)
        before_up = jnp.einsum("gq,qgm->gm", weight_up, collected[:, 1], precision=highest)
        before_down = before_down.reshape(half_groups, rhs.shape[1], rhs.shape[2], 1)
        before_up = before_up.reshape(rhs.shape[0] - half_groups, rhs.shape[1], rhs.shape[2], 1)
        upper_part = solved[:half_groups] + spike_down[:, None, None, :] * before_down
        lower_part = solved[half_groups:] + spike_up[:, None, None, :] * before_up
        current = jnp.concatenate([upper_part, lower_part], axis=0)
    return current


def solution(mesh):
    return jax.shard_map(
        on_device,
        mesh=mesh,
        in_specs=(P(None, None, "stream", "wall"), P(), P(), P(), P("stream", "wall"), P(), P()),
        out_specs=P(None, None, "stream", "wall"),
        check_vma=False,
    )
```

profile of v0, /device:TPU:0, one launch (start us, length us, event | category | flops | bytes accessed | tf_op | source)
XLA Modules:
  0.0 102.3 jit_solution(17074522535210460240)
XLA Ops:
  0.0 2.6 %fusion.112 = (f32[8,64,1,128]{3,2,1,0:T(1,128)S(1)}, f32[8,64,1,128]{3,2,1,0:T(1,128)S(1)}) fusion(f32[8,64,8,128]{3,2,1,0:T(8,128)} %param.7), kind=kLoop, calls=%fused_computation.164 | loop fusion | bytes 1048576 | tf_op jit(solution)/shard_map/slice | solution.py:22
  3.2 2.0 %collective-permute-start.1 = (f32[8,64,1,128]{3,2,1,0:T(1,128)S(1)}, f32[8,64,1,128]{3,2,1,0:T(1,128)S(1)}, u32[]{:S(2)}, u32[]{:S(2)}) collective-permute-start(f32[8,64,1,128]{3,2,1,0:T(1,128)S(1)} %get-tuple-element.22), channel_id=1, source_target_pairs={{1,0},{2,1},{3,2},{0,3},{5,4},{6,5},{7,6},{4,7},{9,8},{10,9},{11,1... | collective-permute-start | bytes 786440 | tf_op jit(solution)/shard_map/ppermute | solution.py:24
  5.2 0.9 slice_reduce_fusion.6
  6.1 1.3 %slice_reduce_fusion.4 = (f32[4,128]{1,0:T(4,128)S(1)}, f32[4,128]{1,0:T(4,128)S(1)}) fusion(f32[8,128,128]{2,1,0:T(8,128)} %param.12), kind=kLoop, calls=%fused_computation.103 | loop fusion | bytes 8192 | tf_op jit(solution)/shard_map/slice | solution.py:53
  7.5 0.7 mul.323
  8.2 0.7 broadcast_maximum_fusion
  8.9 0.7 compare_convert_fusion.1
  9.6 1.5 %broadcast_multiply_fusion.1 = (f32[8,64]{1,0:T(8,128)S(1)}, f32[8,64]{1,0:T(8,128)S(1)}, f32[]{:T(128)}, f32[]{:T(128)}) fusion(f32[8,64]{1,0:T(8,128)} %param.8, f32[64]{0:T(128)} %param.9, f32[8]{0:T(128)} %param.10, f32[64]{0:T(128)S(1)} %get-tuple-element.50, f32[8]{0:T(128)S(1)} %mul.323, f32[64]{0:T(128)S(1)} %get-tuple-element.44), kind=kLoop, calls=%fused_computation.140 | loop fusion | flops 6142 | bytes 6984 | tf_op jit(solution)/shard_map/mul | solution.py:42
  11.0 3.0 %fusion.56 = f32[3,8,128]{2,0,1:T(4,128)S(1)} fusion(f32[8,64,8,128]{3,2,1,0:T(8,128)} %param.7, f32[1,8,64]{2,0,1:T(1,128)S(1)} %bitcast.85, f32[1,8,64]{2,0,1:T(1,128)S(1)} %bitcast.83, f32[1,8,64]{2,0,1:T(1,128)} %bitcast.79), kind=kOutput, calls=%fused_computation.66 | convolution fusion | flops 18877440 | bytes 2115584 | tf_op jit(solution)/shard_map/mgx,gxsw->msw/dot_general | solution.py:56
  14.3 1.3 %fusion.97 = (f32[8,64]{1,0:T(8,128)S(1)}, f32[8,64]{1,0:T(8,128)S(1)}) fusion(f32[]{:T(128)} %get-tuple-element.40, f32[8]{0:T(128)S(1)} %mul.323, f32[64]{0:T(128)S(1)} %get-tuple-element.44, f32[]{:T(128)} %get-tuple-element.39, f32[64]{0:T(128)S(1)} %get-tuple-element.50), kind=kLoop, calls=%fused_computation.132 | loop fusion | flops 4096 | bytes 4648 | tf_op jit(solution)/shard_map/div | solution.py:37
  16.2 1.4 %fusion.30 = f32[1,8,128,1]{2,0,3,1:T(1,128)S(1)} fusion(f32[8,64,1,1]{1,2,0,3:T(1,128)S(1)} %bitcast.80, f32[8,64,8,128]{3,2,1,0:T(8,128)S(1)} %multiply_exponential_fusion.1), kind=kOutput, calls=%fused_computation.38 | convolution fusion | flops 6291456 | bytes 2103296 | tf_op jit(solution)/shard_map/gx,gxsw->sw/dot_general | solution.py:63
  17.6 4.2 %fusion.21 = f32[8,64,8,128]{3,2,1,0:T(8,128)S(1)} fusion(f32[8,64,8,128]{3,2,1,0:T(8,128)S(1)} %copy-done, f32[8,64,1,128]{3,2,1,0:T(1,128)S(1)} %collective-permute-done.1, f32[8,64,1,128]{3,2,1,0:T(1,128)S(1)} %collective-permute-done, f32[8,64]{1,0:T(8,128)S(1)} %get-tuple-element.52, f32[8,128]{1,0:T(8,128)S(1)} %get-tuple-element.42, ...), kind=kOutput, calls=%fused_computation.29 | convolution fusion | flops 817889280 | bytes 5558784 | tf_op jit(solution)/shard_map/gxsj,gij->gxsi/dot_general | solution.py:75
  21.8 0.9 slice_reduce_fusion.3
  23.0 31.6 %all-gather = f32[16,4,512]{2,1,0:T(4,128)S(1)} all-gather(f32[2,4,512]{2,1,0:T(4,128)S(1)} %pad_maximum_fusion.11), channel_id=2, replica_groups=mesh['wall'=8,'stream'=4] {'wall'}, dimensions={0}, use_global_device_ids=true | all-gather | bytes 147456 | tf_op jit(solution)/shard_map/all_gather | solution.py:79
  55.2 0.7 slice_add_fusion.2
  56.5 1.7 %collective-permute-start.3 = (f32[8,64,1,128]{3,2,1,0:T(1,128)S(1)}, f32[8,64,1,128]{3,2,1,0:T(1,128)S(1)}, u32[]{:S(2)}, u32[]{:S(2)}) collective-permute-start(f32[8,64,1,128]{3,2,1,0:T(1,128)S(1)} %get-tuple-element.18), channel_id=1, source_target_pairs={{1,0},{2,1},{3,2},{0,3},{5,4},{6,5},{7,6},{4,7},{9,8},{10,9},{11,1... | collective-permute-start | bytes 786440 | tf_op jit(solution)/shard_map/ppermute | solution.py:24
  58.3 1.4 %fusion.59 = f32[3,8,128]{2,0,1:T(4,128)S(1)} fusion(f32[8,64,8,128]{3,2,1,0:T(8,128)S(1)} %pad_maximum_fusion, f32[1,8,64]{2,0,1:T(1,128)S(1)} %bitcast.86, f32[1,8,64]{2,0,1:T(1,128)S(1)} %bitcast.84, f32[1,8,64]{2,0,1:T(1,128)S(1)} %bitcast.81), kind=kOutput, calls=%fused_computation.67 | convolution fusion | flops 18877440 | bytes 2115584 | tf_op jit(solution)/shard_map/mgx,gxsw->msw/dot_general | solution.py:56
  60.2 1.4 %fusion.28 = f32[1,8,128,1]{2,0,3,1:T(1,128)S(1)} fusion(f32[8,64,1,1]{1,2,0,3:T(1,128)S(1)} %bitcast.82, f32[8,64,8,128]{3,2,1,0:T(8,128)S(1)} %multiply_exponential_fusion), kind=kOutput, calls=%fused_computation.36 | convolution fusion | flops 6291456 | bytes 2103296 | tf_op jit(solution)/shard_map/gx,gxsw->sw/dot_general | solution.py:63
  61.5 1.7 %collective-permute-done.2 = f32[8,64,1,128]{3,2,1,0:T(1,128)S(1)} collective-permute-done((f32[8,64,1,128]{3,2,1,0:T(1,128)S(1)}, f32[8,64,1,128]{3,2,1,0:T(1,128)S(1)}, u32[]{:S(2)}, u32[]{:S(2)}) %collective-permute-start.2) | collective-permute-done | bytes 262176 | tf_op jit(solution)/shard_map/ppermute | solution.py:21
  63.2 0.9 collective-permute-done.3
  64.2 4.2 %fusion.7 = f32[8,64,8,128]{3,2,1,0:T(8,128)S(1)} fusion(f32[8,64,1,128]{3,2,1,0:T(1,128)S(1)} %collective-permute-done.3, f32[4,64,8,128]{3,2,1,0:T(8,128)S(1)} %get-tuple-element.19, f32[4,64,8,128]{3,2,1,0:T(8,128)S(1)} %get-tuple-element.20, f32[8,64,1,128]{3,2,1,0:T(1,128)S(1)} %collective-permute-done.2, f32[8,128]{1,0:T(8,128)S(1)} %bitcast.103, ...), kind=kOutput, calls=%fused_computation.13 | convolution fusion | flops 819462144 | bytes 5558784 | tf_op jit(solution)/shard_map/gxsj,gij->gxsi/dot_general | solution.py:75
  68.3 0.9 slice_reduce_fusion.1
  69.5 30.5 %all-gather.1 = f32[16,4,512]{2,1,0:T(4,128)S(1)} all-gather(f32[2,4,512]{2,1,0:T(4,128)S(1)} %pad_maximum_fusion.12), channel_id=3, replica_groups=mesh['wall'=8,'stream'=4] {'wall'}, dimensions={0}, use_global_device_ids=true | all-gather | bytes 147456 | tf_op jit(solution)/shard_map/all_gather | solution.py:79
  100.7 1.7 %slice_add_fusion.1 = (f32[8,64,8,128]{3,2,1,0:T(8,128)}, f32[8,64,8,128]{3,2,1,0:T(8,128)}) fusion(f32[8,64,8,128]{3,2,1,0:T(8,128)S(1)} %fusion.7, f32[4,64,8]{2,1,0:T(8,128)S(1)} %mul.366, f32[4,128]{1,0:T(4,128)S(1)} %get-tuple-element.56, f32[4,64,8]{2,1,0:T(8,128)S(1)} %mul.369, ...), kind=kLoop, output_to_operand_aliasing={{0}: (5, {}), {1}: (5, {})}, calls=%fused_computation.71 | loop fusion | flops 1048576 | bytes 4214784 | tf_op jit(solution)/shard_map/add | solution.py:96
  (56 shorter events, 4.1 us)
Async XLA Ops:
  0.0 14.1 %copy-start.4 = (f32[8]{0:T(128)S(1)}, f32[8]{0:T(128)}, u32[]{:S(2)}) copy-start(f32[8]{0:T(128)} %param.10) | copy-start | bytes 100
  0.0 14.2 %copy-start.3 = (f32[64]{0:T(128)S(1)}, f32[64]{0:T(128)}, u32[]{:S(2)}) copy-start(f32[64]{0:T(128)} %param.9) | copy-start | bytes 772
  2.7 14.9 %collective-permute-start = (f32[8,64,1,128]{3,2,1,0:T(1,128)S(1)}, f32[8,64,1,128]{3,2,1,0:T(1,128)S(1)}, u32[]{:S(2)}, u32[]{:S(2)}) collective-permute-start(f32[8,64,1,128]{3,2,1,0:T(1,128)S(1)} %get-tuple-element.21), channel_id=1, source_target_pairs={{0,1},{1,2},{2,3},{3,0},{4,5},{5,6},{6,7},{7,4},{8,9},{9,10},{10,1... | collective-permute-start | bytes 786440 | tf_op jit(solution)/shard_map/ppermute | solution.py:21
  3.2 14.4 %collective-permute-start.1 = (f32[8,64,1,128]{3,2,1,0:T(1,128)S(1)}, f32[8,64,1,128]{3,2,1,0:T(1,128)S(1)}, u32[]{:S(2)}, u32[]{:S(2)}) collective-permute-start(f32[8,64,1,128]{3,2,1,0:T(1,128)S(1)} %get-tuple-element.22), channel_id=1, source_target_pairs={{1,0},{2,1},{3,2},{0,3},{5,4},{6,5},{7,6},{4,7},{9,8},{10,9},{11,1... | collective-permute-start | bytes 786440 | tf_op jit(solution)/shard_map/ppermute | solution.py:24
  11.0 4.9 %copy-start.5 = (f32[8]{0:T(128)S(1)}, f32[8]{0:T(128)}, u32[]{:S(2)}) copy-start(f32[8]{0:T(128)} %param.13) | copy-start | bytes 100
  11.0 5.1 %copy-start.2 = (f32[8,64]{1,0:T(8,128)S(1)}, f32[8,64]{1,0:T(8,128)}, u32[]{:S(2)}) copy-start(f32[8,64]{1,0:T(8,128)} %param.8) | copy-start | bytes 6148
  15.6 1.9 %copy-start = (f32[8,64,8,128]{3,2,1,0:T(8,128)S(1)}, f32[8,64,8,128]{3,2,1,0:T(8,128)}, u32[]{:S(2)}) copy-start(f32[8,64,8,128]{3,2,1,0:T(8,128)} %param.7) | copy-start | bytes 6291460
  15.6 1.9 %copy-start.1 = (f32[8,128,128]{2,1,0:T(8,128)S(1)}, f32[8,128,128]{2,1,0:T(8,128)}, u32[]{:S(2)}) copy-start(f32[8,128,128]{2,1,0:T(8,128)} %param.12) | copy-start | bytes 1572868
  56.5 6.8 %collective-permute-start.2 = (f32[8,64,1,128]{3,2,1,0:T(1,128)S(1)}, f32[8,64,1,128]{3,2,1,0:T(1,128)S(1)}, u32[]{:S(2)}, u32[]{:S(2)}) collective-permute-start(f32[8,64,1,128]{3,2,1,0:T(1,128)S(1)} %get-tuple-element.17), channel_id=1, source_target_pairs={{0,1},{1,2},{2,3},{3,0},{4,5},{5,6},{6,7},{7,4},{8,9},{9,10},{10,1... | collective-permute-start | bytes 786440 | tf_op jit(solution)/shard_map/ppermute | solution.py:21
  56.5 7.6 %collective-permute-start.3 = (f32[8,64,1,128]{3,2,1,0:T(1,128)S(1)}, f32[8,64,1,128]{3,2,1,0:T(1,128)S(1)}, u32[]{:S(2)}, u32[]{:S(2)}) collective-permute-start(f32[8,64,1,128]{3,2,1,0:T(1,128)S(1)} %get-tuple-element.18), channel_id=1, source_target_pairs={{1,0},{2,1},{3,2},{0,3},{5,4},{6,5},{7,6},{4,7},{9,8},{10,9},{11,1... | collective-permute-start | bytes 786440 | tf_op jit(solution)/shard_map/ppermute | solution.py:24
where the time goes:
time: 103 us; the launch traced here: 102 us
  blocking collectives  62.1 us (60%)
  matrix products  16.2 us (16%)
  other arithmetic  9.04 us (9%)
  local copies, waits for them, and re-layouts  7.66 us (7%)
  starting transfers between devices  4.31 us (4%)
  waiting for transfers between devices  2.65 us (3%)
    all_gather x2, blocking collectives, on_device(): collected = lax.all_gather(stacked, 'wall', axis=0, tiled=True)  62.1 us
    dot_general x2, matrix products, on_device(): solved = jnp.einsum('gxsj,gij->gxsi', rhs, block_inverse, precision=highest)  8.41 us
    dot_general x2, matrix products, on_device(): jnp.einsum('mgx,gxsw->msw', moment_table, current, precision=highest)  4.36 us
    ppermute x2, starting transfers between devices, with_halo(): lax.ppermute(lax.slice_in_dim(block, 0, width, axis=dim), axis, backward)  3.75 us
    dot_general x2, matrix products, on_device(): zsum = jnp.einsum('gx,gxsw->sw', quad_weight, exponent, precision=highest)  2.72 us
    slice x1, local copies, waits for them, and re-layouts, with_halo(): lax.slice_in_dim(block, block.shape[dim] - width, None, axis=dim)  2.65 us
  transfers between devices with their start and end apart: 4, of which 2 were waited for; matrix products, arithmetic and copies ran while one was open for 15% of the time, Pallas kernels for 0%

commit v1 on v0

v1 whole, which is shorter than its diff:
```python
import functools
import jax
import jax.numpy as jnp
from jax import lax
from jax.experimental import pallas as pl
from jax.experimental.pallas import tpu as pltpu
from jax.sharding import PartitionSpec as P

ITERS = 2
CFL_STREAM = 0.12
RELAX = 0.3
PENALTY = 0.5
INLET_SPEED = 0.5
MESH = pl.DeviceIdType.MESH
F32 = jnp.float32
BF16 = jnp.bfloat16
NT = (((1,), (1,)), ((), ()))
TN = (((0,), (0,)), ((), ()))


def split(value):
    high = value.astype(BF16)
    return high, (value - high.astype(F32)).astype(BF16)


def kernel(
    groups, nx, ns, n_wall, n_stream,
    dist, qw, vx, vy, flags, inv, lc,
    out,
    cur, rhs, packed, weight, end_row, spike, factor, ex, tx, rx, ix, ry, eya,
    edge_l, edge_r, halo_l, halo_r, ends, others, before,
    load_sem, sl_sem, sr_sem, rl_sem, rr_sem, ws_sem, wr_sem,
):
    cw = cur.shape[1]
    half = groups // 2
    rows = nx * ns
    part = ends.shape[3]
    pieces = rows // part
    wall = lax.axis_index("wall")
    stream = lax.axis_index("stream")
    left = lax.rem(stream + n_stream - 1, n_stream)
    right = lax.rem(stream + 1, n_stream)

    loads = [
        pltpu.make_async_copy(
            dist.at[pl.ds(g * rows, rows)], cur.at[pl.ds(g * rows, rows)], load_sem.at[g]
        )
        for g in range(groups)
    ]
    for load in loads:
        load.start()

    barrier = pltpu.get_barrier_semaphore()
    for to in (left, right):
        pl.semaphore_signal(barrier, inc=1, device_id=(wall, to), device_id_type=MESH)
    for step in range(1, n_wall):
        to = lax.rem(wall + step, n_wall)
        pl.semaphore_signal(barrier, inc=1, device_id=(to, stream), device_id_type=MESH)
    pl.semaphore_wait(barrier, 2 + n_wall - 1)

    def halo_copies(it, g):
        here = pl.ds(g * nx, nx)
        return (
            pltpu.make_async_remote_copy(
                src_ref=edge_r.at[it, here], dst_ref=halo_l.at[it, here],
                send_sem=sr_sem.at[it, g], recv_sem=rl_sem.at[it, g],
                device_id=(wall, right), device_id_type=MESH,
            ),
            pltpu.make_async_remote_copy(
                src_ref=edge_l.at[it, here], dst_ref=halo_r.at[it, here],
                send_sem=sl_sem.at[it, g], recv_sem=rr_sem.at[it, g],
                device_id=(wall, left), device_id_type=MESH,
            ),
        )

    def send_edges(it, g):
        here = pl.ds(g * nx, nx)
        edge_r[it, here, :] = cur[pl.ds(g * rows + ns - 1, nx, stride=ns), :]
        edge_l[it, here, :] = cur[pl.ds(g * rows, nx, stride=ns), :]
        for copy in halo_copies(it, g):
            copy.start()

    for g in range(groups):
        loads[g].wait()
        send_edges(0, g)

    zero = jnp.zeros((ns, cw), F32)

    def table_step(x, carry):
        v = jnp.full((ns, cw), vx[x], F32)
        rest = jnp.exp(-0.5 * (v * v))
        shifted = v - INLET_SPEED
        inlet = jnp.exp(-0.5 * (shifted * shifted))
        rx[x] = rest
        ix[x] = inlet
        sums = list(carry)
        for g in range(groups):
            w = qw[g, x]
            sums[g] = sums[g] + w * rest
            sums[groups + g] = sums[groups + g] + w * inlet
        return tuple(sums)

    sums = lax.fori_loop(0, nx, table_step, (zero,) * (2 * groups))
    rest_sum = zero
    inlet_sum = zero
    for g in range(groups):
        v = jnp.full((ns, cw), vy[g], F32)
        factor_y = jnp.exp(-0.5 * (v * v))
        ry[g] = factor_y
        rest_sum = rest_sum + factor_y * sums[g]
        inlet_sum = inlet_sum + factor_y * sums[groups + g]
    kind = flags[...]
    solid = jnp.where(kind == 1, PENALTY, 0.0).astype(F32)
    inflow = jnp.where(kind == 2, PENALTY, 0.0).astype(F32)
    keep = 1.0 - solid - inflow
    solid_part = solid / rest_sum
    inlet_part = inflow / inlet_sum

    row16 = lax.broadcasted_iota(jnp.int32, (16, cw), 0)
    for g in range(groups):
        m = inv[g]
        high, low = split(m)
        weight[g, 0:cw, 0:cw] = high
        weight[g, 0:cw, cw:] = high
        weight[g, cw:, 0:cw] = low
        weight[g, cw:, cw:] = jnp.zeros((cw, cw), BF16)
        mt = m.T
        down = g < half
        last = m[cw - 1 : cw, :] if down else m[0:1, :]
        col = (mt[0:1, :] if down else mt[cw - 1 : cw, :]) * lc[g]
        last_high, last_low = split(last)
        last_high = last_high.astype(F32)
        last_low = last_low.astype(F32)
        end_row[g, :, 0:cw] = jnp.where(
            row16 == 0, last_high, jnp.where(row16 == 1, last_low, 0.0)
        ).astype(BF16)
        end_row[g, :, cw:] = jnp.where(row16 == 0, last_high, 0.0).astype(BF16)
        col_high, col_low = split(col)
        row8 = lax.broadcasted_iota(jnp.int32, (8, cw), 0)
        spike[g] = jnp.where(
            row8 < 2, col_high.astype(F32), jnp.where(row8 == 2, col_low.astype(F32), 0.0)
        )
        one = col[:, cw - 1 : cw] if down else col[:, 0:1]
        side, gg = (0, g) if down else (1, g - half)
        for h in range(pieces):
            factor[side, gg * pieces + h : gg * pieces + h + 1, :] = jnp.broadcast_to(one, (1, part))

    sub = lax.broadcasted_iota(jnp.int32, (ns, cw), 0)
    row8b = lax.broadcasted_iota(jnp.int32, (8, rows), 0)

    for it in range(ITERS):
        def moment_step(x, carry):
            sums = list(carry)
            total = None
            for g in range(groups):
                f = cur[pl.ds(pl.multiple_of(g * rows + x * ns, ns), ns), :]
                wf = qw[g, x] * f
                sums[g] = sums[g] + wf
                total = wf if total is None else total + wf
            sums[groups] = sums[groups] + vx[x] * total
            return tuple(sums)

        sums = lax.fori_loop(0, nx, moment_step, (zero,) * (groups + 1), unroll=2)
        density = sums[0]
        along_y = vy[0] * sums[0]
        for g in range(1, groups):
            density = density + sums[g]
            along_y = along_y + vy[g] * sums[g]
        speed_x = sums[groups] / density
        speed_y = along_y / density
        solid_now = solid_part * density

        def equil_step(x, carry):
            diff = vx[x] - speed_x
            e = jnp.exp(-0.5 * (diff * diff))
            ex[x] = e
            tx[x] = solid_now * rx[x] + inlet_part * ix[x]
            return tuple(carry[g] + qw[g, x] * e for g in range(groups))

        sums = lax.fori_loop(0, nx, equil_step, (zero,) * groups, unroll=2)
        zsum = zero
        vertical = []
        for g in range(groups):
            diff = vy[g] - speed_y
            e = jnp.exp(-0.5 * (diff * diff))
            vertical.append(e)
            zsum = zsum + e * sums[g]
        scale = RELAX * density / zsum
        for g in range(groups):
            eya[g] = scale * vertical[g]

        for g in range(groups):
            for copy in halo_copies(it, g):
                copy.wait()

        def rhs_step(x, carry):
            v = vx[x]
            from_left = CFL_STREAM * jnp.maximum(v, 0.0)
            from_right = CFL_STREAM * jnp.maximum(-v, 0.0)
            stay = keep - (from_left + from_right)
            e = ex[x]
            t = tx[x]
            for g in range(groups):
                here = pl.ds(pl.multiple_of(g * rows + x * ns, ns), ns)
                f = cur[here, :]
                low = halo_l[it, pl.ds(g * nx + x, 1), :]
                high = halo_r[it, pl.ds(g * nx + x, 1), :]
                lower = jnp.where(sub == 0, low, pltpu.roll(f, 1, 0))
                upper = jnp.where(sub == ns - 1, high, pltpu.roll(f, ns - 1, 0))
                rhs[here, :] = (
                    stay * f + from_left * lower + from_right * upper + eya[g] * e + ry[g] * t
                )
            return carry

        lax.fori_loop(0, nx, rhs_step, 0, unroll=2)

        def wall_copy(peer, side):
            return pltpu.make_async_remote_copy(
                src_ref=ends.at[it, side], dst_ref=others.at[it, wall],
                send_sem=ws_sem.at[it, peer], recv_sem=wr_sem.at[it, wall],
                device_id=(peer, stream), device_id_type=MESH,
            )

        def wall_arrival(peer):
            return pltpu.make_async_remote_copy(
                src_ref=ends.at[it, 0], dst_ref=others.at[it, peer],
                send_sem=ws_sem.at[it, peer], recv_sem=wr_sem.at[it, peer],
                device_id=(peer, stream), device_id_type=MESH,
            )

        for side in range(2):
            for gg in range(half):
                g = side * half + gg
                here = pl.ds(g * rows, rows)
                high, low = split(rhs[here, :])
                packed[here, 0:cw] = high
                packed[here, cw:] = low
                two = lax.dot_general(
                    end_row[g], packed[here, :], NT, preferred_element_type=F32
                )
                end = two[0:1, :] + two[1:2, :]
                for h in range(pieces):
                    ends[it, side, gg * pieces + h : gg * pieces + h + 1, :] = end[
                        :, h * part : (h + 1) * part
                    ]
            for peer in range(n_wall):
                @pl.when((peer > wall) if side == 0 else (peer < wall))
                def _():
                    wall_copy(peer, side).start()

        for g in range(groups):
            here = pl.ds(g * rows, rows)
            two = lax.dot_general(
                packed[here, :], weight[g], NT, preferred_element_type=F32
            )
            cur[here, :] = two[:, 0:cw] + two[:, cw:]

        before[...] = jnp.zeros_like(before)
        for peer in range(n_wall):
            @pl.when(peer < wall)
            def _():
                wall_arrival(peer).wait_recv()
                before[0] = factor[0] * before[0] + others[it, peer]
        for peer in reversed(range(n_wall)):
            @pl.when(peer > wall)
            def _():
                wall_arrival(peer).wait_recv()
                before[1] = factor[1] * before[1] + others[it, peer]

        for g in range(groups):
            side, gg = (0, g) if g < half else (1, g - half)
            here = pl.ds(g * rows, rows)
            b = jnp.concatenate(
                [before[side, gg * pieces + h : gg * pieces + h + 1, :] for h in range(pieces)],
                axis=1,
            )
            high, low = split(b)
            high = high.astype(F32)
            low = low.astype(F32)
            left_hand = jnp.where(row8b == 1, low, jnp.where(row8b < 3, high, 0.0))
            value = cur[here, :] + lax.dot_general(
                left_hand, spike[g], TN, preferred_element_type=F32
            )
            if it == ITERS - 1:
                out[here, :] = value
            else:
                cur[here, :] = value
                send_edges(it + 1, g)

        for peer in range(n_wall):
            @pl.when(peer != wall)
            def _():
                wall_arrival(peer).wait_send()


def on_device(n_wall, n_stream, dist, quad_weight, vel_x, vel_y, flags, block_inverse, line_coupling):
    groups, nx, ns, cw = dist.shape
    lines = groups * nx
    total = lines * ns
    rows = nx * ns
    pieces = 8 // (groups // 2)
    part = rows // pieces
    flat = dist.reshape(total, cw)
    smem = pl.BlockSpec(memory_space=pltpu.SMEM)
    vmem = pl.BlockSpec(memory_space=pltpu.VMEM)
    result = pl.pallas_call(
        functools.partial(kernel, groups, nx, ns, n_wall, n_stream),
        out_shape=jax.ShapeDtypeStruct((total, cw), F32),
        in_specs=[pl.BlockSpec(memory_space=pl.ANY), smem, smem, smem, vmem, vmem, smem],
        out_specs=vmem,
        scratch_shapes=[
            pltpu.VMEM((total, cw), F32),
            pltpu.VMEM((total, cw), F32),
            pltpu.VMEM((total, 2 * cw), BF16),
            pltpu.VMEM((groups, 2 * cw, 2 * cw), BF16),
            pltpu.VMEM((groups, 16, 2 * cw), BF16),
            pltpu.VMEM((groups, 8, cw), F32),
            pltpu.VMEM((2, 8, part), F32),
            pltpu.VMEM((nx, ns, cw), F32),
            pltpu.VMEM((nx, ns, cw), F32),
            pltpu.VMEM((nx, ns, cw), F32),
            pltpu.VMEM((nx, ns, cw), F32),
            pltpu.VMEM((groups, ns, cw), F32),
            pltpu.VMEM((groups, ns, cw), F32),
            pltpu.VMEM((ITERS, lines, cw), F32),
            pltpu.VMEM((ITERS, lines, cw), F32),
            pltpu.VMEM((ITERS, lines, cw), F32),
            pltpu.VMEM((ITERS, lines, cw), F32),
            pltpu.VMEM((ITERS, 2, 8, part), F32),
            pltpu.VMEM((ITERS, n_wall, 8, part), F32),
            pltpu.VMEM((2, 8, part), F32),
            pltpu.SemaphoreType.DMA((groups,)),
            pltpu.SemaphoreType.DMA((ITERS, groups)),
            pltpu.SemaphoreType.DMA((ITERS, groups)),
            pltpu.SemaphoreType.DMA((ITERS, groups)),
            pltpu.SemaphoreType.DMA((ITERS, groups)),
            pltpu.SemaphoreType.DMA((ITERS, n_wall)),
            pltpu.SemaphoreType.DMA((ITERS, n_wall)),
        ],
        compiler_params=pltpu.CompilerParams(
            collective_id=0, has_side_effects=True, vmem_limit_bytes=40 * 1024 * 1024
        ),
    )(flat, quad_weight, vel_x, vel_y, flags, block_inverse, line_coupling)
    return result.reshape(groups, nx, ns, cw)


def solution(mesh):
    return jax.shard_map(
        functools.partial(on_device, mesh.shape["wall"], mesh.shape["stream"]),
        mesh=mesh,
        in_specs=(P(None, None, "stream", "wall"), P(), P(), P(), P("stream", "wall"), P(), P()),
        out_specs=P(None, None, "stream", "wall"),
        check_vma=False,
    )
```

time: 103 us -> 42.2 us (0.41)
  blocking collectives: 62.1 us -> 0 us
  Pallas kernels: 0 us -> 34.6 us
  matrix products: 16.2 us -> 0 us
  other arithmetic: 9.04 us -> 0 us
  starting transfers between devices: 4.31 us -> 0 us
  waiting for transfers between devices: 2.65 us -> 0 us
    all_gather x2 -> x0, blocking collectives: 62.1 us -> none  [on_device(): collected = lax.all_gather(stacked, 'wall', axis=0, tiled=True)]
    pallas_call x0 -> x1, Pallas kernels: none -> 34.6 us  [on_device(): pl.pallas_call(functools.partial(kernel, groups, nx, ns, n_wall, n_stream...]
    dot_general x10 -> x0, matrix products: 16.2 us -> none  [the longest x2 8.41 us: on_device(): solved = jnp.einsum('gxsj,gij->gxsi', rhs, block_inverse, precision=highest)]
    unnamed x12 -> x15, local copies, waits for them, and re-layouts: 0.02 us -> 7.29 us
    slice x7 -> x0, local copies, waits for them, and re-layouts: 6.72 us -> none  [the longest x1 2.65 us: with_halo(): lax.slice_in_dim(block, block.shape[dim] - width, None, axis=dim)]
    ppermute x4 -> x0, starting transfers between devices: 4.31 us -> none  [the longest x2 3.75 us: with_halo(): lax.ppermute(lax.slice_in_dim(block, 0, width, axis=dim), axis, backward)]
    mul x7 -> x0, other arithmetic: 2.68 us -> none  [the longest x1 1.45 us: on_device(): quad_weight * vel_x[None, :]]
    ppermute x4 -> x0, waiting for transfers between devices: 2.65 us -> none  [the longest x2 1.72 us: with_halo(): lax.ppermute(lax.slice_in_dim(block, block.shape[dim] - width, None, axis...]
  transfers between devices with their start and end apart: 4 -> 0, of which waited for: 2 -> 0; matrix products, arithmetic and copies ran while one was open for 15% -> 0% of each run, Pallas kernels for 0% -> 0%
where the time goes in v1:
time: 42.2 us; the launch traced here: 41.9 us
  Pallas kernels  34.6 us (82%)
  local copies, waits for them, and re-layouts  7.29 us (17%)
    pallas_call x1, Pallas kernels, on_device(): pl.pallas_call(functools.partial(kernel, groups, nx, ns, n_wall, n_stream...  34.6 us
    unnamed x15, local copies, waits for them, and re-layouts  7.29 us

profile of v1, /device:TPU:0, one launch (start us, length us, event | category | flops | bytes accessed | tf_op | source)
XLA Modules:
  0.0 41.9 jit_solution(18390908585223778608)
XLA Ops:
  0.0 0.0 copy-start
  0.0 1.6 %copy-done = f32[8,64,8,128]{3,2,1,0:T(8,128)S(1)} copy-done((f32[8,64,8,128]{3,2,1,0:T(8,128)S(1)}, f32[8,64,8,128]{3,2,1,0:T(8,128)}, u32[]{:S(2)}) %copy-start) | copy-done | bytes 2097176
  1.6 0.0 copy-start.1
  1.6 1.0 %copy-done.1 = f32[8,128,128]{2,1,0:T(8,128)S(1)} copy-done((f32[8,128,128]{2,1,0:T(8,128)S(1)}, f32[8,128,128]{2,1,0:T(8,128)}, u32[]{:S(2)}) %copy-start.1) | copy-done | bytes 524312
  2.6 0.0 copy-start.2
  2.6 0.7 %copy-done.2 = f32[8,64]{1,0:T(8,128)S(1)} copy-done((f32[8,64]{1,0:T(8,128)S(1)}, f32[8,64]{1,0:T(8,128)}, u32[]{:S(2)}) %copy-start.2) | copy-done | bytes 2072
  3.3 0.0 copy-start.3
  3.3 0.7 %copy-done.3 = s32[8,128]{1,0:T(8,128)S(1)} copy-done((s32[8,128]{1,0:T(8,128)S(1)}, s32[8,128]{1,0:T(8,128)}, u32[]{:S(2)}) %copy-start.3) | copy-done | bytes 4120
  4.0 0.0 copy-start.4
  4.0 0.7 %copy-done.4 = f32[64]{0:T(128)S(1)} copy-done((f32[64]{0:T(128)S(1)}, f32[64]{0:T(128)}, u32[]{:S(2)}) %copy-start.4) | copy-done | bytes 280
  4.7 0.0 copy-start.5
  4.7 0.7 %copy-done.5 = f32[8]{0:T(128)S(1)} copy-done((f32[8]{0:T(128)S(1)}, f32[8]{0:T(128)}, u32[]{:S(2)}) %copy-start.5) | copy-done | bytes 56
  5.3 0.0 copy-start.6
  5.3 0.7 %copy-done.6 = f32[8]{0:T(128)S(1)} copy-done((f32[8]{0:T(128)S(1)}, f32[8]{0:T(128)}, u32[]{:S(2)}) %copy-start.6) | copy-done | bytes 56
  6.0 34.6 %shard_map.73 = f32[4096,128]{1,0:T(8,128)S(1)} custom-call(f32[4096,128]{1,0:T(8,128)S(1)} %bitcast.3, f32[8,64]{1,0:T(8,128)S(1)} %copy-done.2, f32[64]{0:T(128)S(1)} %copy-done.4, f32[8]{0:T(128)S(1)} %copy-done.5, s32[8,128]{1,0:T(8,128)S(1)} %copy-done.3, f32[8,128,128]{2,1,0:T(8,128)S(1)} %copy-done.1, f32[8]{0:T(128)S(1)} %copy-done.6), custom_call_target="tpu_custom_call" | custom-call | tf_op jit(solution)/shard_map/pallas_call | solution.py:306
  40.6 1.3 %copy.9 = f32[8,64,8,128]{3,2,1,0:T(8,128)} copy(f32[8,64,8,128]{3,2,1,0:T(8,128)S(1)} %bitcast.2) | data formatting | bytes 4194304
Async XLA Ops:
  0.0 1.6 %copy-start = (f32[8,64,8,128]{3,2,1,0:T(8,128)S(1)}, f32[8,64,8,128]{3,2,1,0:T(8,128)}, u32[]{:S(2)}) copy-start(f32[8,64,8,128]{3,2,1,0:T(8,128)} %param.7) | copy-start | bytes 6291460
  1.6 1.0 %copy-start.1 = (f32[8,128,128]{2,1,0:T(8,128)S(1)}, f32[8,128,128]{2,1,0:T(8,128)}, u32[]{:S(2)}) copy-start(f32[8,128,128]{2,1,0:T(8,128)} %inv.1) | copy-start | bytes 1572868
  2.6 0.7 %copy-start.2 = (f32[8,64]{1,0:T(8,128)S(1)}, f32[8,64]{1,0:T(8,128)}, u32[]{:S(2)}) copy-start(f32[8,64]{1,0:T(8,128)} %qw.1) | copy-start | bytes 6148
  3.3 0.7 %copy-start.3 = (s32[8,128]{1,0:T(8,128)S(1)}, s32[8,128]{1,0:T(8,128)}, u32[]{:S(2)}) copy-start(s32[8,128]{1,0:T(8,128)} %flags.1) | copy-start | bytes 12292
  4.0 0.7 %copy-start.4 = (f32[64]{0:T(128)S(1)}, f32[64]{0:T(128)}, u32[]{:S(2)}) copy-start(f32[64]{0:T(128)} %vx.1) | copy-start | bytes 772
  4.7 0.7 %copy-start.5 = (f32[8]{0:T(128)S(1)}, f32[8]{0:T(128)}, u32[]{:S(2)}) copy-start(f32[8]{0:T(128)} %vy.1) | copy-start | bytes 100
  5.3 0.7 %copy-start.6 = (f32[8]{0:T(128)S(1)}, f32[8]{0:T(128)}, u32[]{:S(2)}) copy-start(f32[8]{0:T(128)} %lc.1) | copy-start | bytes 100

commit v2 on v1

--- a/solution.py
+++ b/solution.py
@@ -25,11 +25,12 @@
 
 def kernel(
     groups, nx, ns, n_wall, n_stream,
-    dist, qw, vx, vy, flags, inv, lc,
+    dist, qw_in, vx_in, vy_in, flags_in, inv_in, lc_in,
     out,
+    qw, vx, vy, lc, flags, inv, sel, near,
     cur, rhs, packed, weight, end_row, spike, factor, ex, tx, rx, ix, ry, eya,
     edge_l, edge_r, halo_l, halo_r, ends, others, before,
-    load_sem, sl_sem, sr_sem, rl_sem, rr_sem, ws_sem, wr_sem,
+    table_sem, store_sem, ns_sem, nr_sem, load_sem, sl_sem, sr_sem, rl_sem, rr_sem, ws_sem, wr_sem,
 ):
     cw = cur.shape[1]
     half = groups // 2
@@ -49,6 +50,14 @@
     ]
     for load in loads:
         load.start()
+    tables = [
+        pltpu.make_async_copy(source, target, table_sem.at[i])
+        for i, (source, target) in enumerate(
+            ((qw_in, qw), (vx_in, vx), (vy_in, vy), (lc_in, lc), (flags_in, flags), (inv_in, inv))
+        )
+    ]
+    for table in tables:
+        table.start()
 
     barrier = pltpu.get_barrier_semaphore()
     for to in (left, right):
@@ -57,6 +66,13 @@
         to = lax.rem(wall + step, n_wall)
         pl.semaphore_signal(barrier, inc=1, device_id=(to, stream), device_id_type=MESH)
     pl.semaphore_wait(barrier, 2 + n_wall - 1)
+
+    stores = [
+        pltpu.make_async_copy(
+            cur.at[pl.ds(g * rows, rows)], out.at[pl.ds(g * rows, rows)], store_sem.at[g]
+        )
+        for g in range(groups)
+    ]
 
     def halo_copies(it, g):
         here = pl.ds(g * nx, nx)
@@ -84,6 +100,8 @@
         loads[g].wait()
         send_edges(0, g)
 
+    for table in tables:
+        table.wait()
     zero = jnp.zeros((ns, cw), F32)
 
     def table_step(x, carry):
@@ -145,6 +163,24 @@
         for h in range(pieces):
             factor[side, gg * pieces + h : gg * pieces + h + 1, :] = jnp.broadcast_to(one, (1, part))
 
+    lane = lax.broadcasted_iota(jnp.int32, (part, nx), 0)
+    line = lax.broadcasted_iota(jnp.int32, (part, nx), 1)
+    for way, node in enumerate((ns - 1, 0)):
+        for h in range(pieces):
+            wanted = (line * ns + node) == (lane + h * part)
+            sel[way, h] = jnp.where(wanted, 1.0, 0.0).astype(BF16)
+    row8n = lax.broadcasted_iota(jnp.int32, (8, nx), 0)
+
+    def near_copies():
+        return [
+            pltpu.make_async_remote_copy(
+                src_ref=before, dst_ref=near.at[way],
+                send_sem=ns_sem.at[way], recv_sem=nr_sem.at[way],
+                device_id=(wall, to), device_id_type=MESH,
+            )
+            for way, to in enumerate((right, left))
+        ]
+
     sub = lax.broadcasted_iota(jnp.int32, (ns, cw), 0)
     row8b = lax.broadcasted_iota(jnp.int32, (8, rows), 0)
 
@@ -192,6 +228,31 @@
         for g in range(groups):
             for copy in halo_copies(it, g):
                 copy.wait()
+        if it > 0:
+            for copy in near_copies():
+                copy.wait()
+            for way, halo in enumerate((halo_l, halo_r)):
+                picked = []
+                both = near[way].reshape(16, part)
+                high, low = split(both)
+                for h in range(pieces):
+                    picked.append((
+                        jnp.dot(high, sel[way, h], preferred_element_type=F32),
+                        jnp.dot(low, sel[way, h], preferred_element_type=F32),
+                    ))
+                for g in range(groups):
+                    high = low = None
+                    for h in range(pieces):
+                        r = g * pieces + h
+                        p_high = picked[h][0][r : r + 1, :]
+                        p_low = picked[h][1][r : r + 1, :]
+                        high = p_high if high is None else high + p_high
+                        low = p_low if low is None else low + p_low
+                    left_hand = jnp.where(row8n == 1, low, jnp.where(row8n < 3, high, 0.0))
+                    here = pl.ds(g * nx, nx)
+                    halo[it, here, :] = halo[it, here, :] + lax.dot_general(
+                        left_hand, spike[g], TN, preferred_element_type=F32
+                    )
 
         def rhs_step(x, carry):
             v = vx[x]
@@ -254,6 +315,8 @@
                 packed[here, :], weight[g], NT, preferred_element_type=F32
             )
             cur[here, :] = two[:, 0:cw] + two[:, cw:]
+            if it < ITERS - 1:
+                send_edges(it + 1, g)
 
         before[...] = jnp.zeros_like(before)
         for peer in range(n_wall):
@@ -267,6 +330,9 @@
                 wall_arrival(peer).wait_recv()
                 before[1] = factor[1] * before[1] + others[it, peer]
 
+        if it < ITERS - 1:
+            for copy in near_copies():
+                copy.start()
         for g in range(groups):
             side, gg = (0, g) if g < half else (1, g - half)
             here = pl.ds(g * rows, rows)
@@ -281,16 +347,16 @@
             value = cur[here, :] + lax.dot_general(
                 left_hand, spike[g], TN, preferred_element_type=F32
             )
+            cur[here, :] = value
             if it == ITERS - 1:
-                out[here, :] = value
-            else:
-                cur[here, :] = value
-                send_edges(it + 1, g)
+                stores[g].start()
 
         for peer in range(n_wall):
             @pl.when(peer != wall)
             def _():
                 wall_arrival(peer).wait_send()
+    for store in stores:
+        store.wait()
 
 
 def on_device(n_wall, n_stream, dist, quad_weight, vel_x, vel_y, flags, block_inverse, line_coupling):
@@ -301,14 +367,21 @@
     pieces = 8 // (groups // 2)
     part = rows // pieces
     flat = dist.reshape(total, cw)
-    smem = pl.BlockSpec(memory_space=pltpu.SMEM)
-    vmem = pl.BlockSpec(memory_space=pltpu.VMEM)
+    anywhere = pl.BlockSpec(memory_space=pl.ANY)
     result = pl.pallas_call(
         functools.partial(kernel, groups, nx, ns, n_wall, n_stream),
         out_shape=jax.ShapeDtypeStruct((total, cw), F32),
-        in_specs=[pl.BlockSpec(memory_space=pl.ANY), smem, smem, smem, vmem, vmem, smem],
-        out_specs=vmem,
+        in_specs=[anywhere] * 7,
+        out_specs=anywhere,
         scratch_shapes=[
+            pltpu.SMEM((groups, nx), F32),
+            pltpu.SMEM((nx,), F32),
+            pltpu.SMEM((groups,), F32),
+            pltpu.SMEM((groups,), F32),
+            pltpu.VMEM((ns, cw), jnp.int32),
+            pltpu.VMEM((groups, cw, cw), F32),
+            pltpu.VMEM((2, pieces, part, nx), BF16),
+            pltpu.VMEM((2, 2, 8, part), F32),
             pltpu.VMEM((total, cw), F32),
             pltpu.VMEM((total, cw), F32),
             pltpu.VMEM((total, 2 * cw), BF16),
@@ -329,6 +402,10 @@
             pltpu.VMEM((ITERS, 2, 8, part), F32),
             pltpu.VMEM((ITERS, n_wall, 8, part), F32),
             pltpu.VMEM((2, 8, part), F32),
+            pltpu.SemaphoreType.DMA((6,)),
+            pltpu.SemaphoreType.DMA((groups,)),
+            pltpu.SemaphoreType.DMA((2,)),
+            pltpu.SemaphoreType.DMA((2,)),
             pltpu.SemaphoreType.DMA((groups,)),
             pltpu.SemaphoreType.DMA((ITERS, groups)),
             pltpu.SemaphoreType.DMA((ITERS, groups)),
@@ -338,7 +415,7 @@
             pltpu.SemaphoreType.DMA((ITERS, n_wall)),
         ],
         compiler_params=pltpu.CompilerParams(
-            collective_id=0, has_side_effects=True, vmem_limit_bytes=40 * 1024 * 1024
+            collective_id=0, has_side_effects=True, vmem_limit_bytes=63 * 1024 * 1024
         ),
     )(flat, quad_weight, vel_x, vel_y, flags, block_inverse, line_coupling)
     return result.reshape(groups, nx, ns, cw)

time: 42.2 us -> 35.3 us (0.84)
  local copies, waits for them, and re-layouts: 7.29 us -> 3.06 us
  Pallas kernels: 34.6 us -> 32.1 us
    unnamed x15 -> x1, local copies, waits for them, and re-layouts: 7.29 us -> 3.06 us
    pallas_call x1, Pallas kernels: 34.6 us -> 32.1 us  [on_device(): pl.pallas_call(functools.partial(kernel, groups, nx, ns, n_wall, n_stream...]
where the time goes in v2:
time: 35.3 us; the launch traced here: 35.1 us
  Pallas kernels  32.1 us (91%)
  local copies, waits for them, and re-layouts  3.06 us (9%)
    pallas_call x1, Pallas kernels, on_device(): pl.pallas_call(functools.partial(kernel, groups, nx, ns, n_wall, n_stream...  32.1 us
    unnamed x1, local copies, waits for them, and re-layouts  3.06 us

profile of v2, /device:TPU:0, one launch (start us, length us, event | category | flops | bytes accessed | tf_op | source)
XLA Modules:
  0.0 35.1 jit_solution(5785558498502732776)
XLA Ops:
  0.0 32.1 %shard_map.73 = f32[4096,128]{1,0:T(8,128)} custom-call(f32[4096,128]{1,0:T(8,128)} %bitcast.3, f32[8,64]{1,0:T(8,128)} %qw_in.1, f32[64]{0:T(128)} %vx_in.1, f32[8]{0:T(128)} %vy_in.1, s32[8,128]{1,0:T(8,128)} %flags_in.1, f32[8,128,128]{2,1,0:T(8,128)} %inv_in.1, f32[8]{0:T(128)} %lc_in.1), custom_call_target="tpu_custom_call" | custom-call | tf_op jit(solution)/shard_map/pallas_call | solution.py:371
  32.1 3.1 %copy.9 = f32[8,64,8,128]{3,2,1,0:T(8,128)} copy(f32[8,64,8,128]{3,2,1,0:T(8,128)} %bitcast.2) | data formatting | bytes 4194304

commit v3 on v2

--- a/solution.py
+++ b/solution.py
@@ -27,10 +27,10 @@
     groups, nx, ns, n_wall, n_stream,
     dist, qw_in, vx_in, vy_in, flags_in, inv_in, lc_in,
     out,
-    qw, vx, vy, lc, flags, inv, sel, near,
+    qw, vx, vy, lc, flags, inv, sel, near, pull_l, pull_r,
     cur, rhs, packed, weight, end_row, spike, factor, ex, tx, rx, ix, ry, eya,
     edge_l, edge_r, halo_l, halo_r, ends, others, before,
-    table_sem, store_sem, ns_sem, nr_sem, load_sem, sl_sem, sr_sem, rl_sem, rr_sem, ws_sem, wr_sem,
+    table_sem, ns_sem, nr_sem, load_sem, sl_sem, sr_sem, rl_sem, rr_sem, ws_sem, wr_sem,
 ):
     cw = cur.shape[1]
     half = groups // 2
@@ -67,13 +67,6 @@
         pl.semaphore_signal(barrier, inc=1, device_id=(to, stream), device_id_type=MESH)
     pl.semaphore_wait(barrier, 2 + n_wall - 1)
 
-    stores = [
-        pltpu.make_async_copy(
-            cur.at[pl.ds(g * rows, rows)], out.at[pl.ds(g * rows, rows)], store_sem.at[g]
-        )
-        for g in range(groups)
-    ]
-
     def halo_copies(it, g):
         here = pl.ds(g * nx, nx)
         return (
@@ -109,6 +102,8 @@
         rest = jnp.exp(-0.5 * (v * v))
         shifted = v - INLET_SPEED
         inlet = jnp.exp(-0.5 * (shifted * shifted))
+        pull_l[pl.ds(x, 1), :] = CFL_STREAM * jnp.maximum(v[0:1, :], 0.0)
+        pull_r[pl.ds(x, 1), :] = CFL_STREAM * jnp.maximum(-v[0:1, :], 0.0)
         rx[x] = rest
         ix[x] = inlet
         sums = list(carry)
@@ -118,7 +113,7 @@
             sums[groups + g] = sums[groups + g] + w * inlet
         return tuple(sums)
 
-    sums = lax.fori_loop(0, nx, table_step, (zero,) * (2 * groups))
+    sums = lax.fori_loop(0, nx, table_step, (zero,) * (2 * groups), unroll=4)
     rest_sum = zero
     inlet_sum = zero
     for g in range(groups):
@@ -196,7 +191,7 @@
             sums[groups] = sums[groups] + vx[x] * total
             return tuple(sums)
 
-        sums = lax.fori_loop(0, nx, moment_step, (zero,) * (groups + 1), unroll=2)
+        sums = lax.fori_loop(0, nx, moment_step, (zero,) * (groups + 1), unroll=4)
         density = sums[0]
         along_y = vy[0] * sums[0]
         for g in range(1, groups):
@@ -213,7 +208,7 @@
             tx[x] = solid_now * rx[x] + inlet_part * ix[x]
             return tuple(carry[g] + qw[g, x] * e for g in range(groups))
 
-        sums = lax.fori_loop(0, nx, equil_step, (zero,) * groups, unroll=2)
+        sums = lax.fori_loop(0, nx, equil_step, (zero,) * groups, unroll=4)
         zsum = zero
         vertical = []
         for g in range(groups):
@@ -225,55 +220,28 @@
         for g in range(groups):
             eya[g] = scale * vertical[g]
 
-        for g in range(groups):
-            for copy in halo_copies(it, g):
-                copy.wait()
-        if it > 0:
-            for copy in near_copies():
-                copy.wait()
-            for way, halo in enumerate((halo_l, halo_r)):
-                picked = []
-                both = near[way].reshape(16, part)
-                high, low = split(both)
-                for h in range(pieces):
-                    picked.append((
-                        jnp.dot(high, sel[way, h], preferred_element_type=F32),
-                        jnp.dot(low, sel[way, h], preferred_element_type=F32),
-                    ))
-                for g in range(groups):
-                    high = low = None
-                    for h in range(pieces):
-                        r = g * pieces + h
-                        p_high = picked[h][0][r : r + 1, :]
-                        p_low = picked[h][1][r : r + 1, :]
-                        high = p_high if high is None else high + p_high
-                        low = p_low if low is None else low + p_low
-                    left_hand = jnp.where(row8n == 1, low, jnp.where(row8n < 3, high, 0.0))
-                    here = pl.ds(g * nx, nx)
-                    halo[it, here, :] = halo[it, here, :] + lax.dot_general(
-                        left_hand, spike[g], TN, preferred_element_type=F32
-                    )
-
         def rhs_step(x, carry):
             v = vx[x]
             from_left = CFL_STREAM * jnp.maximum(v, 0.0)
             from_right = CFL_STREAM * jnp.maximum(-v, 0.0)
             stay = keep - (from_left + from_right)
+            inner_left = jnp.where(sub == 0, 0.0, from_left)
+            inner_right = jnp.where(sub == ns - 1, 0.0, from_right)
             e = ex[x]
             t = tx[x]
             for g in range(groups):
                 here = pl.ds(pl.multiple_of(g * rows + x * ns, ns), ns)
                 f = cur[here, :]
-                low = halo_l[it, pl.ds(g * nx + x, 1), :]
-                high = halo_r[it, pl.ds(g * nx + x, 1), :]
-                lower = jnp.where(sub == 0, low, pltpu.roll(f, 1, 0))
-                upper = jnp.where(sub == ns - 1, high, pltpu.roll(f, ns - 1, 0))
                 rhs[here, :] = (
-                    stay * f + from_left * lower + from_right * upper + eya[g] * e + ry[g] * t
+                    stay * f
+                    + inner_left * pltpu.roll(f, 1, 0)
+                    + inner_right * pltpu.roll(f, ns - 1, 0)
+                    + eya[g] * e
+                    + ry[g] * t
                 )
             return carry
 
-        lax.fori_loop(0, nx, rhs_step, 0, unroll=2)
+        lax.fori_loop(0, nx, rhs_step, 0, unroll=4)
 
         def wall_copy(peer, side):
             return pltpu.make_async_remote_copy(
@@ -289,10 +257,45 @@
                 device_id=(peer, stream), device_id_type=MESH,
             )
 
+        picks = []
+        if it > 0:
+            for copy in near_copies():
+                copy.wait()
+            for way in range(2):
+                high, low = split(near[way].reshape(16, part))
+                picks.append([
+                    (
+                        jnp.dot(high, sel[way, h], preferred_element_type=F32),
+                        jnp.dot(low, sel[way, h], preferred_element_type=F32),
+                    )
+                    for h in range(pieces)
+                ])
+
+        def add_halo(g):
+            for copy in halo_copies(it, g):
+                copy.wait()
+            for way, (halo, pull) in enumerate(((halo_l, pull_l), (halo_r, pull_r))):
+                value = halo[it, pl.ds(g * nx, nx), :]
+                if it > 0:
+                    high = low = None
+                    for h in range(pieces):
+                        r = g * pieces + h
+                        p_high = picks[way][h][0][r : r + 1, :]
+                        p_low = picks[way][h][1][r : r + 1, :]
+                        high = p_high if high is None else high + p_high
+                        low = p_low if low is None else low + p_low
+                    left_hand = jnp.where(row8n == 1, low, jnp.where(row8n < 3, high, 0.0))
+                    value = value + lax.dot_general(
+                        left_hand, spike[g], TN, preferred_element_type=F32
+                    )
+                edge = pl.ds(g * rows + (0 if way == 0 else ns - 1), nx, stride=ns)
+                rhs[edge, :] = rhs[edge, :] + pull[...] * value
+
         for side in range(2):
             for gg in range(half):
                 g = side * half + gg
                 here = pl.ds(g * rows, rows)
+                add_halo(g)
                 high, low = split(rhs[here, :])
                 packed[here, 0:cw] = high
                 packed[here, cw:] = low
@@ -347,16 +350,15 @@
             value = cur[here, :] + lax.dot_general(
                 left_hand, spike[g], TN, preferred_element_type=F32
             )
-            cur[here, :] = value
             if it == ITERS - 1:
-                stores[g].start()
+                out[here, :] = value
+            else:
+                cur[here, :] = value
 
         for peer in range(n_wall):
             @pl.when(peer != wall)
             def _():
                 wall_arrival(peer).wait_send()
-    for store in stores:
-        store.wait()
 
 
 def on_device(n_wall, n_stream, dist, quad_weight, vel_x, vel_y, flags, block_inverse, line_coupling):
@@ -367,12 +369,13 @@
     pieces = 8 // (groups // 2)
     part = rows // pieces
     flat = dist.reshape(total, cw)
-    anywhere = pl.BlockSpec(memory_space=pl.ANY)
+    hbm = pl.BlockSpec(memory_space=pltpu.HBM)
+    vmem = pl.BlockSpec(memory_space=pltpu.VMEM)
     result = pl.pallas_call(
         functools.partial(kernel, groups, nx, ns, n_wall, n_stream),
-        out_shape=jax.ShapeDtypeStruct((total, cw), F32),
-        in_specs=[anywhere] * 7,
-        out_specs=anywhere,
+        out_shape=pltpu.VMEM((total, cw), F32),
+        in_specs=[hbm] * 7,
+        out_specs=vmem,
         scratch_shapes=[
             pltpu.SMEM((groups, nx), F32),
             pltpu.SMEM((nx,), F32),
@@ -382,6 +385,8 @@
             pltpu.VMEM((groups, cw, cw), F32),
             pltpu.VMEM((2, pieces, part, nx), BF16),
             pltpu.VMEM((2, 2, 8, part), F32),
+            pltpu.VMEM((nx, cw), F32),
+            pltpu.VMEM((nx, cw), F32),
             pltpu.VMEM((total, cw), F32),
             pltpu.VMEM((total, cw), F32),
             pltpu.VMEM((total, 2 * cw), BF16),
@@ -403,7 +408,6 @@
             pltpu.VMEM((ITERS, n_wall, 8, part), F32),
             pltpu.VMEM((2, 8, part), F32),
             pltpu.SemaphoreType.DMA((6,)),
-            pltpu.SemaphoreType.DMA((groups,)),
             pltpu.SemaphoreType.DMA((2,)),
             pltpu.SemaphoreType.DMA((2,)),
             pltpu.SemaphoreType.DMA((groups,)),
@@ -415,7 +419,7 @@
             pltpu.SemaphoreType.DMA((ITERS, n_wall)),
         ],
         compiler_params=pltpu.CompilerParams(
-            collective_id=0, has_side_effects=True, vmem_limit_bytes=63 * 1024 * 1024
+            collective_id=0, has_side_effects=True, vmem_limit_bytes=52 * 1024 * 1024
         ),
     )(flat, quad_weight, vel_x, vel_y, flags, block_inverse, line_coupling)
     return result.reshape(groups, nx, ns, cw)

time: 35.3 us -> 31.7 us (0.90)
  Pallas kernels: 32.1 us -> 30.2 us
  local copies, waits for them, and re-layouts: 3.06 us -> 1.32 us
    pallas_call x1, Pallas kernels: 32.1 us -> 30.2 us  [on_device(): pl.pallas_call(functools.partial(kernel, groups, nx, ns, n_wall, n_stream...]
    unnamed x1, local copies, waits for them, and re-layouts: 3.06 us -> 1.32 us
where the time goes in v3:
time: 31.7 us; the launch traced here: 31.5 us
  Pallas kernels  30.2 us (95%)
  local copies, waits for them, and re-layouts  1.32 us (4%)
    pallas_call x1, Pallas kernels, on_device(): pl.pallas_call(functools.partial(kernel, groups, nx, ns, n_wall, n_stream...  30.2 us
    unnamed x1, local copies, waits for them, and re-layouts  1.32 us

profile of v3, /device:TPU:0, one launch (start us, length us, event | category | flops | bytes accessed | tf_op | source)
XLA Modules:
  0.0 31.5 jit_solution(1751256834899329861)
XLA Ops:
  0.0 30.2 %shard_map.73 = f32[4096,128]{1,0:T(8,128)S(1)} custom-call(f32[4096,128]{1,0:T(8,128)} %bitcast.3, f32[8,64]{1,0:T(8,128)} %qw_in.1, f32[64]{0:T(128)} %vx_in.1, f32[8]{0:T(128)} %vy_in.1, s32[8,128]{1,0:T(8,128)} %flags_in.1, f32[8,128,128]{2,1,0:T(8,128)} %inv_in.1, f32[8]{0:T(128)} %lc_in.1), custom_call_target="tpu_custom_call" | custom-call | tf_op jit(solution)/shard_map/pallas_call | solution.py:374
  30.2 1.3 %copy.9 = f32[8,64,8,128]{3,2,1,0:T(8,128)} copy(f32[8,64,8,128]{3,2,1,0:T(8,128)S(1)} %bitcast.2) | data formatting | bytes 4194304

commit v4 on v3

--- a/solution.py
+++ b/solution.py
@@ -132,12 +132,12 @@
     row16 = lax.broadcasted_iota(jnp.int32, (16, cw), 0)
     for g in range(groups):
         m = inv[g]
-        high, low = split(m)
+        mt = m.T
+        high, low = split(mt)
         weight[g, 0:cw, 0:cw] = high
-        weight[g, 0:cw, cw:] = high
-        weight[g, cw:, 0:cw] = low
+        weight[g, cw:, 0:cw] = high
+        weight[g, 0:cw, cw:] = low
         weight[g, cw:, cw:] = jnp.zeros((cw, cw), BF16)
-        mt = m.T
         down = g < half
         last = m[cw - 1 : cw, :] if down else m[0:1, :]
         col = (mt[0:1, :] if down else mt[cw - 1 : cw, :]) * lc[g]
@@ -191,7 +191,7 @@
             sums[groups] = sums[groups] + vx[x] * total
             return tuple(sums)
 
-        sums = lax.fori_loop(0, nx, moment_step, (zero,) * (groups + 1), unroll=4)
+        sums = lax.fori_loop(0, nx, moment_step, (zero,) * (groups + 1), unroll=8)
         density = sums[0]
         along_y = vy[0] * sums[0]
         for g in range(1, groups):
@@ -208,7 +208,7 @@
             tx[x] = solid_now * rx[x] + inlet_part * ix[x]
             return tuple(carry[g] + qw[g, x] * e for g in range(groups))
 
-        sums = lax.fori_loop(0, nx, equil_step, (zero,) * groups, unroll=4)
+        sums = lax.fori_loop(0, nx, equil_step, (zero,) * groups, unroll=8)
         zsum = zero
         vertical = []
         for g in range(groups):
@@ -314,9 +314,7 @@
 
         for g in range(groups):
             here = pl.ds(g * rows, rows)
-            two = lax.dot_general(
-                packed[here, :], weight[g], NT, preferred_element_type=F32
-            )
+            two = jnp.dot(packed[here, :], weight[g], preferred_element_type=F32)
             cur[here, :] = two[:, 0:cw] + two[:, cw:]
             if it < ITERS - 1:
                 send_edges(it + 1, g)

time: 31.7 us -> 31.7 us (level)
  no operation moved by 1% of the time
where the time goes in v4:
time: 31.7 us; the launch traced here: 31.6 us
  Pallas kernels  30.2 us (95%)
  local copies, waits for them, and re-layouts  1.32 us (4%)
    pallas_call x1, Pallas kernels, on_device(): pl.pallas_call(functools.partial(kernel, groups, nx, ns, n_wall, n_stream...  30.2 us
    unnamed x1, local copies, waits for them, and re-layouts  1.32 us

profile of v4, /device:TPU:0, one launch (start us, length us, event | category | flops | bytes accessed | tf_op | source)
XLA Modules:
  0.0 31.6 jit_solution(11998491438108768968)
XLA Ops:
  0.0 30.2 %shard_map.73 = f32[4096,128]{1,0:T(8,128)S(1)} custom-call(f32[4096,128]{1,0:T(8,128)} %bitcast.3, f32[8,64]{1,0:T(8,128)} %qw_in.1, f32[64]{0:T(128)} %vx_in.1, f32[8]{0:T(128)} %vy_in.1, s32[8,128]{1,0:T(8,128)} %flags_in.1, f32[8,128,128]{2,1,0:T(8,128)} %inv_in.1, f32[8]{0:T(128)} %lc_in.1), custom_call_target="tpu_custom_call" | custom-call | tf_op jit(solution)/shard_map/pallas_call | solution.py:372
  30.2 1.3 %copy.9 = f32[8,64,8,128]{3,2,1,0:T(8,128)} copy(f32[8,64,8,128]{3,2,1,0:T(8,128)S(1)} %bitcast.2) | data formatting | bytes 4194304
